TPU v7x, 256 devices: a whole 4x4x8 slice. The times are simulated.
256 devices in a mesh: row: 16 (over z, y_hi), col: 16 (over y_lo, x, core).
Axes of the slice: x: 4, y: 4 (y_hi: 2, y_lo: 2; y = y_hi * 2 + y_lo), z: 8, core: 2. Of those that a mesh axis runs over, the one named last changes fastest.
Arguments:
- amplitudes: bfloat16 [8192, 49152], P('row', 'col'), may hold values from -6 to 6
- amp_mask: int32 [64, 384], P('row', 'col'), may hold values 0 or 1
- integrals: bfloat16 [49152, 2048], P(('col', 'row')), may hold values from -0.109375 to 0.109375
- int_mask: int32 [384, 16], replicated, may hold values 0 or 1
- others: float32 [2048, 8192], P('col', 'row'), may hold values from -6 to 6
- occ_energy: float32 [8192], P('row'), may hold values from -3 to -0.5
- virt_energy: float32 [2048], P('col'), may hold values from 0.5 to 3
Outputs:
- update: float32 [2048, 8192], P('col', 'row')
All inputs are finite; a program needn't handle non-finite values. No bound on the sum of `amp_mask` on one device may be relied on, other than what follows from the above.
Results may differ from a plain program's by a relative error of at most 0.0003.
Values may be sent and summed in bfloat16 or wider, within the bound.
No kernel may reach another device: no remote copies, remote signals or barrier semaphores. Data moves between devices by JAX's collectives and lax.ppermute only.
A program may use at most 64 MiB of HBM per device.

v0:
```python
import functools

import jax
import jax.numpy as jnp
from jax import lax
from jax.experimental import pallas as pl
from jax.experimental.pallas import tpu as pltpu
from jax.sharding import Mesh, PartitionSpec as P

TILE = 128
HALF = 64
NZ, NX = 8, 4
OFFSETS = (0, -1, 1, -2, 2, -3, 3, 4)
CHAINS = (
    ((1, 0), (3, 0), (2, 0), (2, 1)),
    ((1, 1), (3, 1), (0, 1), (0, 0)),
)
BF16, F32 = jnp.bfloat16, jnp.float32
VMEM_LIMIT = 16 * 1024 * 1024


def whole(space=pltpu.VMEM):
    return pl.BlockSpec(memory_space=space)


def params():
    return pltpu.CompilerParams(vmem_limit_bytes=VMEM_LIMIT)


def column_of():
    return (lax.axis_index("yl") * NX + lax.axis_index("x")) * 2 + lax.axis_index("c")


def keep_where(flag, value):
    return jnp.where(flag != 0, value, jnp.zeros_like(value))


def integral_kernel(mask_ref, in_ref, send_ref, *own_refs):
    yh, yl = lax.axis_index("yh"), lax.axis_index("yl")
    x, c = lax.axis_index("x"), lax.axis_index("c")
    full_rows = pl.ds(pl.multiple_of(yh * HALF, HALF), TILE)
    half_rows = pl.ds(pl.multiple_of((1 - yh) * TILE, HALF), HALF)
    for flip in (1, 0):
        core = lax.rem(c + flip, 2)
        sent = 0
        for chain, slots in enumerate(CHAINS):
            for slot, (dx, other) in enumerate(slots):
                tile = (lax.rem(yl + other, 2) * NX + lax.rem(x + dx, NX)) * 2 + core
                source = pl.ds(pl.multiple_of(tile * TILE, TILE), TILE)
                out_ref, place = (send_ref, sent) if flip else (own_refs[chain], slot)
                target = pl.ds(place * TILE, TILE)
                out_ref[:TILE, target] = keep_where(mask_ref[2 * yh, tile], in_ref[full_rows, source])
                out_ref[TILE:, target] = keep_where(mask_ref[1, tile], in_ref[half_rows, source])
                sent += 1


def prepare_integrals(integrals, int_mask):
    rows, window = integrals.shape
    first_tile = 24 * column_of() + 3 * lax.axis_index("z")
    mask_rows = lax.dynamic_slice_in_dim(int_mask, first_tile, 3, axis=0)
    widths = (window // 2,) + tuple(TILE * len(slots) for slots in CHAINS)
    outs = pl.pallas_call(
        integral_kernel,
        out_shape=tuple(jax.ShapeDtypeStruct((rows, width), BF16) for width in widths),
        in_specs=[whole(pltpu.SMEM), whole()],
        out_specs=(whole(),) * len(widths),
        compiler_params=params(),
        cost_estimate=pl.CostEstimate(flops=0, bytes_accessed=2 * rows * window * 2, transcendentals=0),
        name="prepare_integrals",
    )(mask_rows, integrals)
    return outs[0], outs[1:]


def amplitude_kernel(flip, mask_ref, in_ref, out_ref):
    z, block = lax.axis_index("z"), pl.program_id(0)
    yh = lax.rem(lax.axis_index("yh") + flip, 2)
    low = lax.broadcasted_iota(jnp.int32, (TILE, TILE), 1) < HALF

    def tile(index):
        columns = pl.ds(pl.multiple_of(index * TILE, TILE), TILE)
        return keep_where(mask_ref[block, index], in_ref[:, columns])

    sources = [lax.rem(z + (offset + NZ), NZ) for offset in OFFSETS]
    for place, zz in enumerate(sources):
        out_ref[:, pl.ds(place * TILE, TILE)] = tile(3 * zz + 2 * yh)
    for pair in range(NZ // 2):
        first, second = (tile(3 * zz + 1).astype(F32) for zz in sources[2 * pair : 2 * pair + 2])
        left = jnp.where(low, first, pltpu.roll(second, HALF, 1))
        right = jnp.where(low, pltpu.roll(first, HALF, 1), second)
        out_ref[:, pl.ds((NZ + pair) * TILE, TILE)] = jnp.where(yh == 0, left, right).astype(BF16)


def prepare_amplitudes(amplitudes, amp_mask, flip):
    rows, columns = amplitudes.shape
    return pl.pallas_call(
        functools.partial(amplitude_kernel, flip),
        grid=(rows // TILE,),
        out_shape=jax.ShapeDtypeStruct((rows, columns // 2), BF16),
        in_specs=[whole(pltpu.SMEM), pl.BlockSpec((TILE, columns), lambda i: (i, 0))],
        out_specs=pl.BlockSpec((TILE, columns // 2), lambda i: (i, 0)),
        compiler_params=params(),
        cost_estimate=pl.CostEstimate(flops=0, bytes_accessed=3 * rows * columns, transcendentals=0),
        name="prepare_amplitudes",
    )(amp_mask, amplitudes)


def product_kernel(half, joined, *refs):
    amps, pieces, outs, held = refs[:2], refs[2 : 2 + NZ], refs[2 + NZ : -1], refs[-1]
    rows, width = pieces[0].shape[0] // 2, held.shape[2]
    columns = pl.ds(half * width, width)
    for place, piece in enumerate(pieces):
        for group in range(2):
            start = group * rows
            full, rest = pl.ds(place * TILE, TILE), pl.ds(NZ * TILE + place * HALF, HALF)
            held[group, full, :] = piece[pl.ds(start, TILE), columns]
            held[group, rest, :] = piece[pl.ds(start + TILE, HALF), columns]
    rows = amps[0].shape[0] // 2
    for side in range(2):
        mine = pl.ds(side * rows, rows)
        total = jnp.dot(amps[0][mine, :], held[0], preferred_element_type=F32)
        total += jnp.dot(amps[1][mine, :], held[1], preferred_element_type=F32)
        for slot in range(2):
            part = total[:, slot * TILE : (slot + 1) * TILE]
            if joined:
                outs[slot][side] = part
            else:
                outs[2 * side + slot][...] = part


def product(amps, pieces, half, joined=False, name="product"):
    rows, depth = amps[0].shape
    rows, width = rows // 2, 2 * TILE
    if joined:
        out_shape = (jax.ShapeDtypeStruct((2, rows, TILE), F32),) * 2
    else:
        out_shape = (jax.ShapeDtypeStruct((rows, TILE), F32),) * 4
    operands = list(amps) + list(pieces)
    outs = pl.pallas_call(
        functools.partial(product_kernel, half, joined),
        out_shape=out_shape,
        in_specs=[whole()] * len(operands),
        out_specs=(whole(),) * len(out_shape),
        scratch_shapes=[pltpu.VMEM((2, depth, width), BF16)],
        compiler_params=params(),
        cost_estimate=pl.CostEstimate(
            flops=8 * rows * depth * width, bytes_accessed=8 * rows * depth, transcendentals=0
        ),
        name=name,
    )(*operands)
    return outs if joined else (outs[:2], outs[2:])


def finish_kernel(*refs):
    totals, (others_ref, occ_ref, virt_ref, out_ref) = refs[:-4], refs[-4:]
    total = totals[0][...]
    for ref in totals[1:]:
        total = total + ref[...]
    virt = jnp.broadcast_to(virt_ref[...], (TILE, TILE)).T
    for block in range(out_ref.shape[1] // TILE):
        columns = pl.ds(block * TILE, TILE)
        ladder = total[block * TILE : (block + 1) * TILE, :].T
        out_ref[:, columns] = (others_ref[:, columns] + ladder) / (virt - occ_ref[:, columns])


def finish(totals, others, occ_energy, virt_energy):
    return pl.pallas_call(
        finish_kernel,
        out_shape=jax.ShapeDtypeStruct(others.shape, F32),
        in_specs=[whole()] * (len(totals) + 3),
        out_specs=whole(),
        compiler_params=params(),
        name="finish",
    )(*totals, others, occ_energy[None, :], virt_energy[None, :])


def shift(value, axis, size, step):
    return lax.ppermute(value, axis, [(i, (i + step) % size) for i in range(size)])


def swap_y(value, bits):
    return lax.ppermute(value, ("yh", "yl"), [(i, i ^ bits) for i in range(4)])


def along_x(value, step):
    return shift(value, "x", NX, step)


def after(value, *others):
    return lax.optimization_barrier((value, *others))[0]


def body(amplitudes, amp_mask, integrals, int_mask, others, occ_energy, virt_energy):
    def join(*values):
        return jnp.concatenate(values, axis=0)

    send, own = prepare_integrals(integrals, int_mask)
    received = shift(send, "c", 2, 1)
    width = own[0].shape[1]
    starts = [join(own[i], received[:, i * width : (i + 1) * width]) for i in range(2)]
    away = prepare_amplitudes(amplitudes, after(amp_mask, *starts), 1)
    keep = prepare_amplitudes(amplitudes, after(amp_mask, away), 0)
    other_rows = swap_y(away, 2)

    chains = [[start] for start in starts]
    ends = [[start, start] for start in starts]
    for step in range(3):
        ends = [[shift(up, "z", NZ, 1), shift(down, "z", NZ, -1)] for up, down in ends]
        if step == 0:
            ends = [[after(up, away, keep), after(down, away, keep)] for up, down in ends]
        for chain, pair in zip(chains, ends):
            chain.extend(pair)
    mine = after(join(other_rows, keep), *ends[0], *ends[1])
    chains[0].append(shift(ends[0][0], "z", NZ, 1))
    chains[1].append(shift(ends[1][1], "z", NZ, -1))
    amps = mine, shift(mine, "c", 2, 1)

    c_there, c_here = [
        (along_x(low, 1), along_x(high, -1))
        for low, high in product(amps, chains[0], 0, name="product_c")
    ]
    up, down = product(amps, chains[1], 0, joined=True, name="product_b")
    near = along_x(up, 1), along_x(down, -1)
    a_there, a_here = product(amps, chains[0], 1, name="product_a")
    far = a_here[0] + swap_y(a_here[1], 1) + swap_y(a_there[1], 3) + swap_y(a_there[0], 2)
    far = along_x(far, 2)
    d_there, d_here = product(amps, chains[1], 1, name="product_d")
    totals = [
        d_here[1],
        far,
        *c_here,
        swap_y(d_there[1] + c_there[0] + c_there[1], 2),
        swap_y(d_here[0] + near[0][1] + near[1][1], 1),
        swap_y(d_there[0] + near[0][0] + near[1][0], 3),
    ]
    return finish(totals, others, occ_energy, virt_energy)


def solution(mesh):
    fine = Mesh(mesh.devices.reshape(NZ, 2, 2, NX, 2), ("z", "yh", "yl", "x", "c"))
    row, col = ("z", "yh"), ("yl", "x", "c")
    placed = (P(row, col), P(row, col), P(col + row, None), P(), P(col, row), P(row), P(col))
    return jax.shard_map(
        body, mesh=fine, in_specs=placed, out_specs=P(col, row), check_vma=False
    )
```

profile of v0, /device:TPU:16, one launch (start us, length us, event | category | flops | bytes accessed | tf_op | source)
XLA Modules:
  0.0 117.0 jit_solution(13617206118233764513)
XLA Ops:
  0.0 0.7 copy-done
  0.7 0.1 constant_dynamic-slice_fusion
  0.8 0.1 copy.9.mask_ref
  0.9 1.2 %copy-done.2 = bf16[192,2048]{1,0:T(8,128)(2,1)S(1)} copy-done((bf16[192,2048]{1,0:T(8,128)(2,1)S(1)}, bf16[192,2048]{1,0:T(8,128)(2,1)}, u32[]{:S(2)}) %copy-start.2) | copy-done | bytes 786456
  2.1 0.8 prepare_integrals.1
  2.9 0.1 collective-permute-start
  3.0 1.7 %collective-permute-done = bf16[192,1024]{1,0:T(8,128)(2,1)S(1)} collective-permute-done((bf16[192,1024]{1,0:T(8,128)(2,1)S(1)}, bf16[192,1024]{1,0:T(8,128)(2,1)S(1)}, u32[]{:S(2)}, u32[]{:S(2)}) %collective-permute-start) | collective-permute-done | bytes 393248 | tf_op jit(solution)/shard_map/ppermute | solution.py:177
  4.9 1.6 %prepare_amplitudes.2 = bf16[512,1536]{1,0:T(8,128)(2,1)S(1)} custom-call(s32[4,24]{1,0:T(4,128)S(1)} %copy-done.4, bf16[512,3072]{1,0:T(8,128)(2,1)S(1)} %copy-done.1), custom_call_target="tpu_custom_call" | custom-call | bytes 4718592 | tf_op jit(solution)/shard_map/prepare_amplitudes/pallas_call | solution.py:95
  6.5 2.2 %collective-permute-start.1 = (bf16[512,1536]{1,0:T(8,128)(2,1)S(1)}, bf16[512,1536]{1,0:T(8,128)(2,1)S(1)}, u32[]{:S(2)}, u32[]{:S(2)}) collective-permute-start(bf16[512,1536]{1,0:T(8,128)(2,1)S(1)} %prepare_amplitudes.2), channel_id=1, source_target_pairs={{0,16},{8,24},{16,0},{24,8},{1,17},{9,25},{17,1},{25,9},{2,18},{10... | collective-permute-start | bytes 4718600 | tf_op jit(solution)/shard_map/ppermute | solution.py:181
  8.6 0.2 collective-permute-start.8
  8.8 3.9 %collective-permute-start.11 = (bf16[384,512]{1,0:T(8,128)(2,1)S(1)}, bf16[384,512]{1,0:T(8,128)(2,1)S(1)}, u32[]{:S(2)}, u32[]{:S(2)}) collective-permute-start(bf16[384,512]{1,0:T(8,128)(2,1)S(1)} %pad_maximum_fusion.2.refs_2_), channel_id=1, source_target_pairs={{0,224},{32,0},{64,32},{96,64},{128,96},{160,128},{192,160},{224,1... | collective-permute-start | bytes 1179656 | tf_op jit(solution)/shard_map/ppermute | solution.py:177
  12.7 2.0 %collective-permute-start.5 = (bf16[384,512]{1,0:T(8,128)(2,1)S(1)}, bf16[384,512]{1,0:T(8,128)(2,1)S(1)}, u32[]{:S(2)}, u32[]{:S(2)}) collective-permute-start(bf16[384,512]{1,0:T(8,128)(2,1)S(1)} %pad_maximum_fusion.1.refs_2_), channel_id=1, source_target_pairs={{0,224},{32,0},{64,32},{96,64},{128,96},{160,128},{192,160},{224,1... | collective-permute-start | bytes 1179656 | tf_op jit(solution)/shard_map/ppermute | solution.py:177
  14.8 1.6 %prepare_amplitudes.3 = bf16[512,1536]{1,0:T(8,128)(2,1)S(1)} custom-call(s32[4,24]{1,0:T(4,128)S(1)} %copy-done.4, bf16[512,3072]{1,0:T(8,128)(2,1)S(1)} %copy-done.1), custom_call_target="tpu_custom_call" | custom-call | bytes 4718592 | tf_op jit(solution)/shard_map/prepare_amplitudes/pallas_call | solution.py:95
  16.3 6.3 %collective-permute-done.8.refs_3_ = bf16[384,512]{1,0:T(8,128)(2,1)S(1)} collective-permute-done((bf16[384,512]{1,0:T(8,128)(2,1)S(1)}, bf16[384,512]{1,0:T(8,128)(2,1)S(1)}, u32[]{:S(2)}, u32[]{:S(2)}) %collective-permute-start.8) | collective-permute-done | bytes 393248 | tf_op jit(solution)/shard_map/ppermute | solution.py:177
  22.7 0.0 collective-permute-start.9
  22.7 0.0 collective-permute-done.11.refs_4_
  22.7 3.3 %collective-permute-start.12 = (bf16[384,512]{1,0:T(8,128)(2,1)S(1)}, bf16[384,512]{1,0:T(8,128)(2,1)S(1)}, u32[]{:S(2)}, u32[]{:S(2)}) collective-permute-start(bf16[384,512]{1,0:T(8,128)(2,1)S(1)} %collective-permute-done.11.refs_4_), channel_id=1, source_target_pairs={{0,224},{32,0},{64,32},{96,64},{128,96},{160,128},{192,160},{224,1... | collective-permute-start | bytes 1179656 | tf_op jit(solution)/shard_map/ppermute | solution.py:177
  25.9 4.7 %collective-permute-done.5.refs_4_ = bf16[384,512]{1,0:T(8,128)(2,1)S(1)} collective-permute-done((bf16[384,512]{1,0:T(8,128)(2,1)S(1)}, bf16[384,512]{1,0:T(8,128)(2,1)S(1)}, u32[]{:S(2)}, u32[]{:S(2)}) %collective-permute-start.5) | collective-permute-done | bytes 393248 | tf_op jit(solution)/shard_map/ppermute | solution.py:177
  30.7 3.7 %collective-permute-start.6 = (bf16[384,512]{1,0:T(8,128)(2,1)S(1)}, bf16[384,512]{1,0:T(8,128)(2,1)S(1)}, u32[]{:S(2)}, u32[]{:S(2)}) collective-permute-start(bf16[384,512]{1,0:T(8,128)(2,1)S(1)} %collective-permute-done.5.refs_4_), channel_id=1, source_target_pairs={{0,224},{32,0},{64,32},{96,64},{128,96},{160,128},{192,160},{224,1... | collective-permute-start | bytes 1179656 | tf_op jit(solution)/shard_map/ppermute | solution.py:177
  34.4 0.0 collective-permute-done.2.refs_3_
  34.4 5.2 %collective-permute-done.9.refs_5_ = bf16[384,512]{1,0:T(8,128)(2,1)S(1)} collective-permute-done((bf16[384,512]{1,0:T(8,128)(2,1)S(1)}, bf16[384,512]{1,0:T(8,128)(2,1)S(1)}, u32[]{:S(2)}, u32[]{:S(2)}) %collective-permute-start.9) | collective-permute-done | bytes 393248 | tf_op jit(solution)/shard_map/ppermute | solution.py:177
  39.5 0.0 collective-permute-start.10
  39.5 0.0 collective-permute-done.12.refs_6_
  39.5 3.3 %collective-permute-start.13 = (bf16[384,512]{1,0:T(8,128)(2,1)S(1)}, bf16[384,512]{1,0:T(8,128)(2,1)S(1)}, u32[]{:S(2)}, u32[]{:S(2)}) collective-permute-start(bf16[384,512]{1,0:T(8,128)(2,1)S(1)} %collective-permute-done.12.refs_6_), channel_id=1, source_target_pairs={{0,224},{32,0},{64,32},{96,64},{128,96},{160,128},{192,160},{224,1... | collective-permute-start | bytes 1179656 | tf_op jit(solution)/shard_map/ppermute | solution.py:177
  42.8 4.7 %collective-permute-done.6.refs_6_ = bf16[384,512]{1,0:T(8,128)(2,1)S(1)} collective-permute-done((bf16[384,512]{1,0:T(8,128)(2,1)S(1)}, bf16[384,512]{1,0:T(8,128)(2,1)S(1)}, u32[]{:S(2)}, u32[]{:S(2)}) %collective-permute-start.6) | collective-permute-done | bytes 393248 | tf_op jit(solution)/shard_map/ppermute | solution.py:177
  47.5 3.7 %collective-permute-start.7 = (bf16[384,512]{1,0:T(8,128)(2,1)S(1)}, bf16[384,512]{1,0:T(8,128)(2,1)S(1)}, u32[]{:S(2)}, u32[]{:S(2)}) collective-permute-start(bf16[384,512]{1,0:T(8,128)(2,1)S(1)} %collective-permute-done.6.refs_6_), channel_id=1, source_target_pairs={{0,224},{32,0},{64,32},{96,64},{128,96},{160,128},{192,160},{224,1... | collective-permute-start | bytes 1179656 | tf_op jit(solution)/shard_map/ppermute | solution.py:177
  51.2 0.0 collective-permute-start.4
  51.2 0.0 collective-permute-done.1
  51.2 0.2 pad_maximum_fusion.refs_0_
  51.4 4.9 %collective-permute-done.10.refs_7_ = bf16[384,512]{1,0:T(8,128)(2,1)S(1)} collective-permute-done((bf16[384,512]{1,0:T(8,128)(2,1)S(1)}, bf16[384,512]{1,0:T(8,128)(2,1)S(1)}, u32[]{:S(2)}, u32[]{:S(2)}) %collective-permute-start.10) | collective-permute-done | bytes 393248 | tf_op jit(solution)/shard_map/ppermute | solution.py:177
  56.4 7.0 %collective-permute-done.7.refs_8_ = bf16[384,512]{1,0:T(8,128)(2,1)S(1)} collective-permute-done((bf16[384,512]{1,0:T(8,128)(2,1)S(1)}, bf16[384,512]{1,0:T(8,128)(2,1)S(1)}, u32[]{:S(2)}, u32[]{:S(2)}) %collective-permute-start.7) | collective-permute-done | bytes 393248 | tf_op jit(solution)/shard_map/ppermute | solution.py:177
  63.4 0.7 collective-permute-done.4.refs_7_
  64.0 0.0 collective-permute-start.16
  64.1 3.2 %collective-permute-start.15 = (bf16[384,512]{1,0:T(8,128)(2,1)S(1)}, bf16[384,512]{1,0:T(8,128)(2,1)S(1)}, u32[]{:S(2)}, u32[]{:S(2)}) collective-permute-start(bf16[384,512]{1,0:T(8,128)(2,1)S(1)} %collective-permute-done.13.refs_8_), channel_id=1, source_target_pairs={{0,224},{32,0},{64,32},{96,64},{128,96},{160,128},{192,160},{224,1... | collective-permute-start | bytes 1179656 | tf_op jit(solution)/shard_map/ppermute | solution.py:177
  67.3 9.6 %collective-permute-done.16.refs_9_ = bf16[384,512]{1,0:T(8,128)(2,1)S(1)} collective-permute-done((bf16[384,512]{1,0:T(8,128)(2,1)S(1)}, bf16[384,512]{1,0:T(8,128)(2,1)S(1)}, u32[]{:S(2)}, u32[]{:S(2)}) %collective-permute-start.16) | collective-permute-done | bytes 393248 | tf_op jit(solution)/shard_map/ppermute | solution.py:177
  76.9 1.8 %product_c.1 = (f32[512,128]{1,0:T(8,128)S(1)}, f32[512,128]{1,0:T(8,128)S(1)}, f32[512,128]{1,0:T(8,128)S(1)}, f32[512,128]{1,0:T(8,128)S(1)}) custom-call(bf16[1024,1536]{1,0:T(8,128)(2,1)S(1)} %pad_maximum_fusion.refs_0_, bf16[1024,1536]{1,0:T(8,128)(2,1)S(1)} %collective-permute-done.14.refs_1_, bf16[384,512]{1,0:T(8,128)(2,1)S(1)} %pad_maximum_fusion.1.refs_2_, ...), custom_call_target="tpu_custom_call" | custom-call | flops 1610612736 | bytes 6291456 | tf_op jit(solution)/shard_map/product_c/pallas_call | solution.py:138
  78.7 1.6 %collective-permute-start.23 = (f32[512,128]{1,0:T(8,128)S(1)}, f32[512,128]{1,0:T(8,128)S(1)}, u32[]{:S(2)}, u32[]{:S(2)}) collective-permute-start(f32[512,128]{1,0:T(8,128)S(1)} %get-tuple-element.47), channel_id=1, source_target_pairs={{0,2},{2,4},{4,6},{6,0},{1,3},{3,5},{5,7},{7,1},{8,10},{10,12},{12... | collective-permute-start | bytes 786440 | tf_op jit(solution)/shard_map/ppermute | solution.py:177
  80.2 1.7 %collective-permute-start.24 = (f32[512,128]{1,0:T(8,128)S(1)}, f32[512,128]{1,0:T(8,128)S(1)}, u32[]{:S(2)}, u32[]{:S(2)}) collective-permute-start(f32[512,128]{1,0:T(8,128)S(1)} %get-tuple-element.48), channel_id=1, source_target_pairs={{0,6},{2,0},{4,2},{6,4},{1,7},{3,1},{5,3},{7,5},{8,14},{10,8},{12,... | collective-permute-start | bytes 786440 | tf_op jit(solution)/shard_map/ppermute | solution.py:177
  82.0 1.8 %product_b.1 = (f32[2,512,128]{2,1,0:T(8,128)S(1)}, f32[2,512,128]{2,1,0:T(8,128)S(1)}) custom-call(bf16[1024,1536]{1,0:T(8,128)(2,1)S(1)} %pad_maximum_fusion.refs_0_, bf16[1024,1536]{1,0:T(8,128)(2,1)S(1)} %collective-permute-done.14.refs_1_, bf16[384,512]{1,0:T(8,128)(2,1)S(1)} %pad_maximum_fusion.2.refs_2_, ...), custom_call_target="tpu_custom_call" | custom-call | flops 1610612736 | bytes 6291456 | tf_op jit(solution)/shard_map/product_b/pallas_call | solution.py:138
  83.8 0.4 collective-permute-start.26
  84.1 3.0 %collective-permute-start.27 = (f32[2,512,128]{2,1,0:T(8,128)S(1)}, f32[2,512,128]{2,1,0:T(8,128)S(1)}, u32[]{:S(2)}, u32[]{:S(2)}) collective-permute-start(f32[2,512,128]{2,1,0:T(8,128)S(1)} %get-tuple-element.51), channel_id=1, source_target_pairs={{0,6},{2,0},{4,2},{6,4},{1,7},{3,1},{5,3},{7,5},{8,14},{10,8},{12,... | collective-permute-start | bytes 1572872 | tf_op jit(solution)/shard_map/ppermute | solution.py:177
  87.1 1.8 %product_a.1 = (f32[512,128]{1,0:T(8,128)S(1)}, f32[512,128]{1,0:T(8,128)S(1)}, f32[512,128]{1,0:T(8,128)S(1)}, f32[512,128]{1,0:T(8,128)S(1)}) custom-call(bf16[1024,1536]{1,0:T(8,128)(2,1)S(1)} %pad_maximum_fusion.refs_0_, bf16[1024,1536]{1,0:T(8,128)(2,1)S(1)} %collective-permute-done.14.refs_1_, bf16[384,512]{1,0:T(8,128)(2,1)S(1)} %pad_maximum_fusion.1.refs_2_, ...), custom_call_target="tpu_custom_call" | custom-call | flops 1610612736 | bytes 6291456 | tf_op jit(solution)/shard_map/product_a/pallas_call | solution.py:138
  88.9 2.1 %collective-permute-start.17 = (f32[512,128]{1,0:T(8,128)S(1)}, f32[512,128]{1,0:T(8,128)S(1)}, u32[]{:S(2)}, u32[]{:S(2)}) collective-permute-start(f32[512,128]{1,0:T(8,128)S(1)} %get-tuple-element.41), channel_id=1, source_target_pairs={{0,8},{8,0},{16,24},{24,16},{1,9},{9,1},{17,25},{25,17},{2,10},{10... | collective-permute-start | bytes 786440 | tf_op jit(solution)/shard_map/ppermute | solution.py:181
  91.0 1.6 %collective-permute-start.18 = (f32[512,128]{1,0:T(8,128)S(1)}, f32[512,128]{1,0:T(8,128)S(1)}, u32[]{:S(2)}, u32[]{:S(2)}) collective-permute-start(f32[512,128]{1,0:T(8,128)S(1)} %get-tuple-element.42), channel_id=1, source_target_pairs={{0,24},{8,16},{16,8},{24,0},{1,25},{9,17},{17,9},{25,1},{2,26},{10... | collective-permute-start | bytes 786440 | tf_op jit(solution)/shard_map/ppermute | solution.py:181
  92.6 0.6 collective-permute-start.19
  93.2 1.8 %product_d.1 = (f32[512,128]{1,0:T(8,128)S(1)}, f32[512,128]{1,0:T(8,128)S(1)}, f32[512,128]{1,0:T(8,128)S(1)}, f32[512,128]{1,0:T(8,128)S(1)}) custom-call(bf16[1024,1536]{1,0:T(8,128)(2,1)S(1)} %pad_maximum_fusion.refs_0_, bf16[1024,1536]{1,0:T(8,128)(2,1)S(1)} %collective-permute-done.14.refs_1_, bf16[384,512]{1,0:T(8,128)(2,1)S(1)} %pad_maximum_fusion.2.refs_2_, ...), custom_call_target="tpu_custom_call" | custom-call | flops 1610612736 | bytes 6291456 | tf_op jit(solution)/shard_map/product_d/pallas_call | solution.py:138
  95.0 0.0 copy-start.3
  95.0 0.0 copy-start.5
  95.0 0.0 copy-start.6
  95.1 3.2 %collective-permute-done.17 = f32[512,128]{1,0:T(8,128)S(1)} collective-permute-done((f32[512,128]{1,0:T(8,128)S(1)}, f32[512,128]{1,0:T(8,128)S(1)}, u32[]{:S(2)}, u32[]{:S(2)}) %collective-permute-start.17) | collective-permute-done | bytes 262176 | tf_op jit(solution)/shard_map/ppermute | solution.py:181
  98.3 4.0 %collective-permute-done.18 = f32[512,128]{1,0:T(8,128)S(1)} collective-permute-done((f32[512,128]{1,0:T(8,128)S(1)}, f32[512,128]{1,0:T(8,128)S(1)}, u32[]{:S(2)}, u32[]{:S(2)}) %collective-permute-start.18) | collective-permute-done | bytes 262176 | tf_op jit(solution)/shard_map/ppermute | solution.py:181
  102.3 0.3 collective-permute-start.22
  102.6 0.6 collective-permute-done.19
  103.2 3.2 %collective-permute-start.25 = (f32[512,128]{1,0:T(8,128)S(1)}, f32[512,128]{1,0:T(8,128)S(1)}, u32[]{:S(2)}, u32[]{:S(2)}) collective-permute-start(f32[512,128]{1,0:T(8,128)S(1)} %add_add_fusion), channel_id=1, source_target_pairs={{0,16},{8,24},{16,0},{24,8},{1,17},{9,25},{17,1},{25,9},{2,18},{10... | collective-permute-start | bytes 786440 | tf_op jit(solution)/shard_map/ppermute | solution.py:181
  106.5 1.0 collective-permute-start.20
  107.5 0.1 fusion
  107.6 0.8 collective-permute-start.28
  108.4 0.3 collective-permute-start.29
  108.7 1.2 %collective-permute-done.22.refs_3_ = f32[512,128]{1,0:T(8,128)S(1)} collective-permute-done((f32[512,128]{1,0:T(8,128)S(1)}, f32[512,128]{1,0:T(8,128)S(1)}, u32[]{:S(2)}, u32[]{:S(2)}) %collective-permute-start.22) | collective-permute-done | bytes 262176 | tf_op jit(solution)/shard_map/ppermute | solution.py:177
  109.9 3.6 %collective-permute-done.25.refs_4_ = f32[512,128]{1,0:T(8,128)S(1)} collective-permute-done((f32[512,128]{1,0:T(8,128)S(1)}, f32[512,128]{1,0:T(8,128)S(1)}, u32[]{:S(2)}, u32[]{:S(2)}) %collective-permute-start.25) | collective-permute-done | bytes 262176 | tf_op jit(solution)/shard_map/ppermute | solution.py:181
  113.5 1.0 collective-permute-done.20.refs_1_
  114.5 0.6 collective-permute-done.28.refs_5_
  115.1 1.1 collective-permute-done.29.refs_6_
  116.2 0.9 finish.1
  (27 shorter events, 0.2 us)
Async XLA Ops:
  0.0 0.7 copy-start
  0.0 4.9 %copy-start.1 = (bf16[512,3072]{1,0:T(8,128)(2,1)S(1)}, bf16[512,3072]{1,0:T(8,128)(2,1)}, u32[]{:S(2)}) copy-start(bf16[512,3072]{1,0:T(8,128)(2,1)} %in_ref.5) | copy-start | bytes 9437188
  0.9 1.2 %copy-start.2 = (bf16[192,2048]{1,0:T(8,128)(2,1)S(1)}, bf16[192,2048]{1,0:T(8,128)(2,1)}, u32[]{:S(2)}) copy-start(bf16[192,2048]{1,0:T(8,128)(2,1)} %in_ref.3) | copy-start | bytes 2359300
  2.1 2.8 %copy-start.4 = (s32[4,24]{1,0:T(4,128)S(1)}, s32[4,24]{1,0:T(4,128)}, u32[]{:S(2)}) copy-start(s32[4,24]{1,0:T(4,128)} %mask_ref.1) | copy-start | bytes 1156
  2.9 1.8 %collective-permute-start = (bf16[192,1024]{1,0:T(8,128)(2,1)S(1)}, bf16[192,1024]{1,0:T(8,128)(2,1)S(1)}, u32[]{:S(2)}, u32[]{:S(2)}) collective-permute-start(bf16[192,1024]{1,0:T(8,128)(2,1)S(1)} %get-tuple-element.30), channel_id=1, source_target_pairs={{0,1},{1,0},{2,3},{3,2},{4,5},{5,4},{6,7},{7,6},{8,9},{9,8},{10,11... | collective-permute-start | bytes 1179656 | tf_op jit(solution)/shard_map/ppermute | solution.py:177
  6.5 44.8 %collective-permute-start.1 = (bf16[512,1536]{1,0:T(8,128)(2,1)S(1)}, bf16[512,1536]{1,0:T(8,128)(2,1)S(1)}, u32[]{:S(2)}, u32[]{:S(2)}) collective-permute-start(bf16[512,1536]{1,0:T(8,128)(2,1)S(1)} %prepare_amplitudes.2), channel_id=1, source_target_pairs={{0,16},{8,24},{16,0},{24,8},{1,17},{9,25},{17,1},{25,9},{2,18},{10... | collective-permute-start | bytes 4718600 | tf_op jit(solution)/shard_map/ppermute | solution.py:181
  8.6 14.1 %collective-permute-start.8 = (bf16[384,512]{1,0:T(8,128)(2,1)S(1)}, bf16[384,512]{1,0:T(8,128)(2,1)S(1)}, u32[]{:S(2)}, u32[]{:S(2)}) collective-permute-start(bf16[384,512]{1,0:T(8,128)(2,1)S(1)} %pad_maximum_fusion.2.refs_2_), channel_id=1, source_target_pairs={{0,32},{32,64},{64,96},{96,128},{128,160},{160,192},{192,224},{224... | collective-permute-start | bytes 1179656 | tf_op jit(solution)/shard_map/ppermute | solution.py:177
  8.8 13.9 %collective-permute-start.11 = (bf16[384,512]{1,0:T(8,128)(2,1)S(1)}, bf16[384,512]{1,0:T(8,128)(2,1)S(1)}, u32[]{:S(2)}, u32[]{:S(2)}) collective-permute-start(bf16[384,512]{1,0:T(8,128)(2,1)S(1)} %pad_maximum_fusion.2.refs_2_), channel_id=1, source_target_pairs={{0,224},{32,0},{64,32},{96,64},{128,96},{160,128},{192,160},{224,1... | collective-permute-start | bytes 1179656 | tf_op jit(solution)/shard_map/ppermute | solution.py:177
  12.7 17.9 %collective-permute-start.5 = (bf16[384,512]{1,0:T(8,128)(2,1)S(1)}, bf16[384,512]{1,0:T(8,128)(2,1)S(1)}, u32[]{:S(2)}, u32[]{:S(2)}) collective-permute-start(bf16[384,512]{1,0:T(8,128)(2,1)S(1)} %pad_maximum_fusion.1.refs_2_), channel_id=1, source_target_pairs={{0,224},{32,0},{64,32},{96,64},{128,96},{160,128},{192,160},{224,1... | collective-permute-start | bytes 1179656 | tf_op jit(solution)/shard_map/ppermute | solution.py:177
  14.8 19.6 %collective-permute-start.2 = (bf16[384,512]{1,0:T(8,128)(2,1)S(1)}, bf16[384,512]{1,0:T(8,128)(2,1)S(1)}, u32[]{:S(2)}, u32[]{:S(2)}) collective-permute-start(bf16[384,512]{1,0:T(8,128)(2,1)S(1)} %pad_maximum_fusion.1.refs_2_), channel_id=1, source_target_pairs={{0,32},{32,64},{64,96},{96,128},{128,160},{160,192},{192,224},{224... | collective-permute-start | bytes 1179656 | tf_op jit(solution)/shard_map/ppermute | solution.py:177
  22.7 16.9 %collective-permute-start.9 = (bf16[384,512]{1,0:T(8,128)(2,1)S(1)}, bf16[384,512]{1,0:T(8,128)(2,1)S(1)}, u32[]{:S(2)}, u32[]{:S(2)}) collective-permute-start(bf16[384,512]{1,0:T(8,128)(2,1)S(1)} %collective-permute-done.8.refs_3_), channel_id=1, source_target_pairs={{0,32},{32,64},{64,96},{96,128},{128,160},{160,192},{192,224},{224... | collective-permute-start | bytes 1179656 | tf_op jit(solution)/shard_map/ppermute | solution.py:177
  22.7 16.9 %collective-permute-start.12 = (bf16[384,512]{1,0:T(8,128)(2,1)S(1)}, bf16[384,512]{1,0:T(8,128)(2,1)S(1)}, u32[]{:S(2)}, u32[]{:S(2)}) collective-permute-start(bf16[384,512]{1,0:T(8,128)(2,1)S(1)} %collective-permute-done.11.refs_4_), channel_id=1, source_target_pairs={{0,224},{32,0},{64,32},{96,64},{128,96},{160,128},{192,160},{224,1... | collective-permute-start | bytes 1179656 | tf_op jit(solution)/shard_map/ppermute | solution.py:177
  30.7 16.9 %collective-permute-start.6 = (bf16[384,512]{1,0:T(8,128)(2,1)S(1)}, bf16[384,512]{1,0:T(8,128)(2,1)S(1)}, u32[]{:S(2)}, u32[]{:S(2)}) collective-permute-start(bf16[384,512]{1,0:T(8,128)(2,1)S(1)} %collective-permute-done.5.refs_4_), channel_id=1, source_target_pairs={{0,224},{32,0},{64,32},{96,64},{128,96},{160,128},{192,160},{224,1... | collective-permute-start | bytes 1179656 | tf_op jit(solution)/shard_map/ppermute | solution.py:177
  34.4 16.9 %collective-permute-start.3 = (bf16[384,512]{1,0:T(8,128)(2,1)S(1)}, bf16[384,512]{1,0:T(8,128)(2,1)S(1)}, u32[]{:S(2)}, u32[]{:S(2)}) collective-permute-start(bf16[384,512]{1,0:T(8,128)(2,1)S(1)} %collective-permute-done.2.refs_3_), channel_id=1, source_target_pairs={{0,32},{32,64},{64,96},{96,128},{128,160},{160,192},{192,224},{224... | collective-permute-start | bytes 1179656 | tf_op jit(solution)/shard_map/ppermute | solution.py:177
  39.5 16.9 %collective-permute-start.10 = (bf16[384,512]{1,0:T(8,128)(2,1)S(1)}, bf16[384,512]{1,0:T(8,128)(2,1)S(1)}, u32[]{:S(2)}, u32[]{:S(2)}) collective-permute-start(bf16[384,512]{1,0:T(8,128)(2,1)S(1)} %collective-permute-done.9.refs_5_), channel_id=1, source_target_pairs={{0,32},{32,64},{64,96},{96,128},{128,160},{160,192},{192,224},{224... | collective-permute-start | bytes 1179656 | tf_op jit(solution)/shard_map/ppermute | solution.py:177
  39.5 16.8 %collective-permute-start.13 = (bf16[384,512]{1,0:T(8,128)(2,1)S(1)}, bf16[384,512]{1,0:T(8,128)(2,1)S(1)}, u32[]{:S(2)}, u32[]{:S(2)}) collective-permute-start(bf16[384,512]{1,0:T(8,128)(2,1)S(1)} %collective-permute-done.12.refs_6_), channel_id=1, source_target_pairs={{0,224},{32,0},{64,32},{96,64},{128,96},{160,128},{192,160},{224,1... | collective-permute-start | bytes 1179656 | tf_op jit(solution)/shard_map/ppermute | solution.py:177
  47.5 15.9 %collective-permute-start.7 = (bf16[384,512]{1,0:T(8,128)(2,1)S(1)}, bf16[384,512]{1,0:T(8,128)(2,1)S(1)}, u32[]{:S(2)}, u32[]{:S(2)}) collective-permute-start(bf16[384,512]{1,0:T(8,128)(2,1)S(1)} %collective-permute-done.6.refs_6_), channel_id=1, source_target_pairs={{0,224},{32,0},{64,32},{96,64},{128,96},{160,128},{192,160},{224,1... | collective-permute-start | bytes 1179656 | tf_op jit(solution)/shard_map/ppermute | solution.py:177
  51.2 12.8 %collective-permute-start.4 = (bf16[384,512]{1,0:T(8,128)(2,1)S(1)}, bf16[384,512]{1,0:T(8,128)(2,1)S(1)}, u32[]{:S(2)}, u32[]{:S(2)}) collective-permute-start(bf16[384,512]{1,0:T(8,128)(2,1)S(1)} %collective-permute-done.3.refs_5_), channel_id=1, source_target_pairs={{0,32},{32,64},{64,96},{96,128},{128,160},{160,192},{192,224},{224... | collective-permute-start | bytes 1179656 | tf_op jit(solution)/shard_map/ppermute | solution.py:177
  64.0 12.8 %collective-permute-start.14 = (bf16[1024,1536]{1,0:T(8,128)(2,1)S(1)}, bf16[1024,1536]{1,0:T(8,128)(2,1)S(1)}, u32[]{:S(2)}, u32[]{:S(2)}) collective-permute-start(bf16[1024,1536]{1,0:T(8,128)(2,1)S(1)} %pad_maximum_fusion.refs_0_), channel_id=1, source_target_pairs={{0,1},{1,0},{2,3},{3,2},{4,5},{5,4},{6,7},{7,6},{8,9},{9,8},{10,11... | collective-permute-start | bytes 9437192 | tf_op jit(solution)/shard_map/ppermute | solution.py:177
  64.0 12.8 %collective-permute-start.16 = (bf16[384,512]{1,0:T(8,128)(2,1)S(1)}, bf16[384,512]{1,0:T(8,128)(2,1)S(1)}, u32[]{:S(2)}, u32[]{:S(2)}) collective-permute-start(bf16[384,512]{1,0:T(8,128)(2,1)S(1)} %collective-permute-done.4.refs_7_), channel_id=1, source_target_pairs={{0,32},{32,64},{64,96},{96,128},{128,160},{160,192},{192,224},{224... | collective-permute-start | bytes 1179656 | tf_op jit(solution)/shard_map/ppermute | solution.py:177
  64.1 17.9 %collective-permute-start.15 = (bf16[384,512]{1,0:T(8,128)(2,1)S(1)}, bf16[384,512]{1,0:T(8,128)(2,1)S(1)}, u32[]{:S(2)}, u32[]{:S(2)}) collective-permute-start(bf16[384,512]{1,0:T(8,128)(2,1)S(1)} %collective-permute-done.13.refs_8_), channel_id=1, source_target_pairs={{0,224},{32,0},{64,32},{96,64},{128,96},{160,128},{192,160},{224,1... | collective-permute-start | bytes 1179656 | tf_op jit(solution)/shard_map/ppermute | solution.py:177
  78.7 12.4 %collective-permute-start.23 = (f32[512,128]{1,0:T(8,128)S(1)}, f32[512,128]{1,0:T(8,128)S(1)}, u32[]{:S(2)}, u32[]{:S(2)}) collective-permute-start(f32[512,128]{1,0:T(8,128)S(1)} %get-tuple-element.47), channel_id=1, source_target_pairs={{0,2},{2,4},{4,6},{6,0},{1,3},{3,5},{5,7},{7,1},{8,10},{10,12},{12... | collective-permute-start | bytes 786440 | tf_op jit(solution)/shard_map/ppermute | solution.py:177
  80.2 12.4 %collective-permute-start.24 = (f32[512,128]{1,0:T(8,128)S(1)}, f32[512,128]{1,0:T(8,128)S(1)}, u32[]{:S(2)}, u32[]{:S(2)}) collective-permute-start(f32[512,128]{1,0:T(8,128)S(1)} %get-tuple-element.48), channel_id=1, source_target_pairs={{0,6},{2,0},{4,2},{6,4},{1,7},{3,1},{5,3},{7,5},{8,14},{10,8},{12,... | collective-permute-start | bytes 786440 | tf_op jit(solution)/shard_map/ppermute | solution.py:177
  83.8 22.7 %collective-permute-start.26 = (f32[2,512,128]{2,1,0:T(8,128)S(1)}, f32[2,512,128]{2,1,0:T(8,128)S(1)}, u32[]{:S(2)}, u32[]{:S(2)}) collective-permute-start(f32[2,512,128]{2,1,0:T(8,128)S(1)} %get-tuple-element.50), channel_id=1, source_target_pairs={{0,2},{2,4},{4,6},{6,0},{1,3},{3,5},{5,7},{7,1},{8,10},{10,12},{12... | collective-permute-start | bytes 1572872 | tf_op jit(solution)/shard_map/ppermute | solution.py:177
  84.1 23.3 %collective-permute-start.27 = (f32[2,512,128]{2,1,0:T(8,128)S(1)}, f32[2,512,128]{2,1,0:T(8,128)S(1)}, u32[]{:S(2)}, u32[]{:S(2)}) collective-permute-start(f32[2,512,128]{2,1,0:T(8,128)S(1)} %get-tuple-element.51), channel_id=1, source_target_pairs={{0,6},{2,0},{4,2},{6,4},{1,7},{3,1},{5,3},{7,5},{8,14},{10,8},{12,... | collective-permute-start | bytes 1572872 | tf_op jit(solution)/shard_map/ppermute | solution.py:177
  88.9 9.4 %collective-permute-start.17 = (f32[512,128]{1,0:T(8,128)S(1)}, f32[512,128]{1,0:T(8,128)S(1)}, u32[]{:S(2)}, u32[]{:S(2)}) collective-permute-start(f32[512,128]{1,0:T(8,128)S(1)} %get-tuple-element.41), channel_id=1, source_target_pairs={{0,8},{8,0},{16,24},{24,16},{1,9},{9,1},{17,25},{25,17},{2,10},{10... | collective-permute-start | bytes 786440 | tf_op jit(solution)/shard_map/ppermute | solution.py:181
  91.0 11.3 %collective-permute-start.18 = (f32[512,128]{1,0:T(8,128)S(1)}, f32[512,128]{1,0:T(8,128)S(1)}, u32[]{:S(2)}, u32[]{:S(2)}) collective-permute-start(f32[512,128]{1,0:T(8,128)S(1)} %get-tuple-element.42), channel_id=1, source_target_pairs={{0,24},{8,16},{16,8},{24,0},{1,25},{9,17},{17,9},{25,1},{2,26},{10... | collective-permute-start | bytes 786440 | tf_op jit(solution)/shard_map/ppermute | solution.py:181
  92.6 10.6 %collective-permute-start.19 = (f32[512,128]{1,0:T(8,128)S(1)}, f32[512,128]{1,0:T(8,128)S(1)}, u32[]{:S(2)}, u32[]{:S(2)}) collective-permute-start(f32[512,128]{1,0:T(8,128)S(1)} %get-tuple-element.43), channel_id=1, source_target_pairs={{0,16},{8,24},{16,0},{24,8},{1,17},{9,25},{17,1},{25,9},{2,18},{10... | collective-permute-start | bytes 786440 | tf_op jit(solution)/shard_map/ppermute | solution.py:181
  95.0 21.2 %copy-start.3 = (f32[128,512]{1,0:T(8,128)S(1)}, f32[128,512]{1,0:T(8,128)}, u32[]{:S(2)}) copy-start(f32[128,512]{1,0:T(8,128)} %refs_7_.1) | copy-start | bytes 786436
  95.0 21.1 %copy-start.5 = (f32[512]{0:T(512)S(1)}, f32[512]{0:T(512)}, u32[]{:S(2)}) copy-start(f32[512]{0:T(512)} %param.12) | copy-start | bytes 6148
  95.0 21.1 %copy-start.6 = (f32[128]{0:T(128)S(1)}, f32[128]{0:T(128)}, u32[]{:S(2)}) copy-start(f32[128]{0:T(128)} %param.13) | copy-start | bytes 1540
  98.2 10.1 %collective-permute-start.21 = (f32[512,128]{1,0:T(8,128)S(1)}, f32[512,128]{1,0:T(8,128)S(1)}, u32[]{:S(2)}, u32[]{:S(2)}) collective-permute-start(f32[512,128]{1,0:T(8,128)S(1)} %get-tuple-element.44), channel_id=1, source_target_pairs={{0,2},{2,4},{4,6},{6,0},{1,3},{3,5},{5,7},{7,1},{8,10},{10,12},{12... | collective-permute-start | bytes 786440 | tf_op jit(solution)/shard_map/ppermute | solution.py:177
  102.3 7.6 %collective-permute-start.22 = (f32[512,128]{1,0:T(8,128)S(1)}, f32[512,128]{1,0:T(8,128)S(1)}, u32[]{:S(2)}, u32[]{:S(2)}) collective-permute-start(f32[512,128]{1,0:T(8,128)S(1)} %get-tuple-element.45), channel_id=1, source_target_pairs={{0,6},{2,0},{4,2},{6,4},{1,7},{3,1},{5,3},{7,5},{8,14},{10,8},{12,... | collective-permute-start | bytes 786440 | tf_op jit(solution)/shard_map/ppermute | solution.py:177
  103.2 10.3 %collective-permute-start.25 = (f32[512,128]{1,0:T(8,128)S(1)}, f32[512,128]{1,0:T(8,128)S(1)}, u32[]{:S(2)}, u32[]{:S(2)}) collective-permute-start(f32[512,128]{1,0:T(8,128)S(1)} %add_add_fusion), channel_id=1, source_target_pairs={{0,16},{8,24},{16,0},{24,8},{1,17},{9,25},{17,1},{25,9},{2,18},{10... | collective-permute-start | bytes 786440 | tf_op jit(solution)/shard_map/ppermute | solution.py:181
  106.5 8.0 %collective-permute-start.20 = (f32[512,128]{1,0:T(8,128)S(1)}, f32[512,128]{1,0:T(8,128)S(1)}, u32[]{:S(2)}, u32[]{:S(2)}) collective-permute-start(f32[512,128]{1,0:T(8,128)S(1)} %add_add_fusion.1), channel_id=1, source_target_pairs={{0,4},{2,6},{4,0},{6,2},{1,5},{3,7},{5,1},{7,3},{8,12},{10,14},{12... | collective-permute-start | bytes 786440 | tf_op jit(solution)/shard_map/ppermute | solution.py:177
  107.6 7.5 %collective-permute-start.28 = (f32[512,128]{1,0:T(8,128)S(1)}, f32[512,128]{1,0:T(8,128)S(1)}, u32[]{:S(2)}, u32[]{:S(2)}) collective-permute-start(f32[512,128]{1,0:T(8,128)S(1)} %get-tuple-element.54), channel_id=1, source_target_pairs={{0,8},{8,0},{16,24},{24,16},{1,9},{9,1},{17,25},{25,17},{2,10},{10... | collective-permute-start | bytes 786440 | tf_op jit(solution)/shard_map/ppermute | solution.py:181
  108.4 7.8 %collective-permute-start.29 = (f32[512,128]{1,0:T(8,128)S(1)}, f32[512,128]{1,0:T(8,128)S(1)}, u32[]{:S(2)}, u32[]{:S(2)}) collective-permute-start(f32[512,128]{1,0:T(8,128)S(1)} %get-tuple-element.53), channel_id=1, source_target_pairs={{0,24},{8,16},{16,8},{24,0},{1,25},{9,17},{17,9},{25,1},{2,26},{10... | collective-permute-start | bytes 786440 | tf_op jit(solution)/shard_map/ppermute | solution.py:181
where the time goes:
time: 119 us; the launch traced here: 117 us
  waiting for transfers between devices  60.1 us (51%)
  starting transfers between devices  42.2 us (35%)
  Pallas kernels  12 us (10%)
  local copies, waits for them, and re-layouts  2.14 us (2%)
    ppermute x23, waiting for transfers between devices, shift(): lax.ppermute(value, axis, [(i, (i + step) % size) for i in range(size)])  47.1 us
    ppermute x23, starting transfers between devices, shift(): lax.ppermute(value, axis, [(i, (i + step) % size) for i in range(size)])  31.3 us
    ppermute x7, waiting for transfers between devices, swap_y(): return lax.ppermute(value, ('yh', 'yl'), [(i, i ^ bits) for i in range(4)])  13 us
    ppermute x7, starting transfers between devices, swap_y(): return lax.ppermute(value, ('yh', 'yl'), [(i, i ^ bits) for i in range(4)])  10.8 us
    pallas_call x4, Pallas kernels, product(): pl.pallas_call(functools.partial(product_kernel, half, joined), out_shape...  7.14 us
    pallas_call x2, Pallas kernels, prepare_amplitudes(): pl.pallas_call(functools.partial(amplitude_kernel, flip), grid=(rows // T...  3.14 us
  transfers between devices with their start and end apart: 30, of which 17 were waited for; matrix products, arithmetic and copies ran while one was open for 0% of the time, Pallas kernels for 7%

commit v1 on v0

--- a/solution.py
+++ b/solution.py
@@ -35,39 +35,48 @@
     return jnp.where(flag != 0, value, jnp.zeros_like(value))
 
 
-def integral_kernel(mask_ref, in_ref, send_ref, *own_refs):
+def integral_kernel(mask_ref, in_ref, *refs):
+    (send_ref, *own_refs), kept = refs[:-1], refs[-1]
     yh, yl = lax.axis_index("yh"), lax.axis_index("yl")
     x, c = lax.axis_index("x"), lax.axis_index("c")
     full_rows = pl.ds(pl.multiple_of(yh * HALF, HALF), TILE)
     half_rows = pl.ds(pl.multiple_of((1 - yh) * TILE, HALF), HALF)
+    first_tile = 24 * column_of() + 3 * lax.axis_index("z")
+    index = lax.broadcasted_iota(jnp.int32, mask_ref.shape, 1)
+    for which, row_tile in enumerate((first_tile + 2 * yh, first_tile + 1)):
+        picked = jnp.where(index == row_tile, mask_ref[...], 0).astype(F32)
+        kept[which] = jnp.broadcast_to(jnp.sum(picked, axis=1, keepdims=True), kept.shape[1:])
+
+    def masked(rows, tile, which):
+        columns = pl.ds(pl.multiple_of(tile * TILE, TILE), TILE)
+        return in_ref[rows, columns] * kept[which, pl.ds(tile, 1), :].astype(BF16)
+
     for flip in (1, 0):
         core = lax.rem(c + flip, 2)
         sent = 0
         for chain, slots in enumerate(CHAINS):
             for slot, (dx, other) in enumerate(slots):
                 tile = (lax.rem(yl + other, 2) * NX + lax.rem(x + dx, NX)) * 2 + core
-                source = pl.ds(pl.multiple_of(tile * TILE, TILE), TILE)
                 out_ref, place = (send_ref, sent) if flip else (own_refs[chain], slot)
                 target = pl.ds(place * TILE, TILE)
-                out_ref[:TILE, target] = keep_where(mask_ref[2 * yh, tile], in_ref[full_rows, source])
-                out_ref[TILE:, target] = keep_where(mask_ref[1, tile], in_ref[half_rows, source])
+                out_ref[:TILE, target] = masked(full_rows, tile, 0)
+                out_ref[TILE:, target] = masked(half_rows, tile, 1)
                 sent += 1
 
 
 def prepare_integrals(integrals, int_mask):
     rows, window = integrals.shape
-    first_tile = 24 * column_of() + 3 * lax.axis_index("z")
-    mask_rows = lax.dynamic_slice_in_dim(int_mask, first_tile, 3, axis=0)
     widths = (window // 2,) + tuple(TILE * len(slots) for slots in CHAINS)
     outs = pl.pallas_call(
         integral_kernel,
         out_shape=tuple(jax.ShapeDtypeStruct((rows, width), BF16) for width in widths),
-        in_specs=[whole(pltpu.SMEM), whole()],
+        in_specs=[whole(), whole()],
         out_specs=(whole(),) * len(widths),
+        scratch_shapes=[pltpu.VMEM((2, int_mask.shape[1], TILE), F32)],
         compiler_params=params(),
         cost_estimate=pl.CostEstimate(flops=0, bytes_accessed=2 * rows * window * 2, transcendentals=0),
         name="prepare_integrals",
-    )(mask_rows, integrals)
+    )(int_mask.T, integrals)
     return outs[0], outs[1:]
 
 
@@ -210,8 +219,8 @@
         for chain, pair in zip(chains, ends):
             chain.extend(pair)
     mine = after(join(other_rows, keep), *ends[0], *ends[1])
-    chains[0].append(shift(ends[0][0], "z", NZ, 1))
-    chains[1].append(shift(ends[1][1], "z", NZ, -1))
+    chains[0].append(shift(ends[0][1], "z", NZ, -1))
+    chains[1].append(shift(ends[1][0], "z", NZ, 1))
     amps = mine, shift(mine, "c", 2, 1)
 
     c_there, c_here = [

time: 119 us -> 118 us (level)
  transfers between devices with their start and end apart: 30 -> 30, of which waited for: 17 -> 17; matrix products, arithmetic and copies ran while one was open for 0% -> 0% of each run, Pallas kernels for 7% -> 8%
where the time goes in v1:
time: 118 us; the launch traced here: 116 us
  waiting for transfers between devices  59.5 us (50%)
  starting transfers between devices  42 us (36%)
  Pallas kernels  11.5 us (10%)
  local copies, waits for them, and re-layouts  2.07 us (2%)
    ppermute x23, waiting for transfers between devices, shift(): lax.ppermute(value, axis, [(i, (i + step) % size) for i in range(size)])  46.6 us
    ppermute x23, starting transfers between devices, shift(): lax.ppermute(value, axis, [(i, (i + step) % size) for i in range(size)])  31.1 us
    ppermute x7, waiting for transfers between devices, swap_y(): return lax.ppermute(value, ('yh', 'yl'), [(i, i ^ bits) for i in range(4)])  13 us
    ppermute x7, starting transfers between devices, swap_y(): return lax.ppermute(value, ('yh', 'yl'), [(i, i ^ bits) for i in range(4)])  10.9 us
    pallas_call x4, Pallas kernels, product(): pl.pallas_call(functools.partial(product_kernel, half, joined), out_shape...  7.14 us
    pallas_call x2, Pallas kernels, prepare_amplitudes(): pl.pallas_call(functools.partial(amplitude_kernel, flip), grid=(rows // T...  3.14 us
  transfers between devices with their start and end apart: 30, of which 17 were waited for; matrix products, arithmetic and copies ran while one was open for 0% of the time, Pallas kernels for 8%

profile of v1, /device:TPU:16, one launch (start us, length us, event | category | flops | bytes accessed | tf_op | source)
XLA Modules:
  0.0 115.7 jit_solution(18275493813529936848)
XLA Ops:
  0.0 1.3 %copy-done.1 = bf16[192,2048]{1,0:T(8,128)(2,1)S(1)} copy-done((bf16[192,2048]{1,0:T(8,128)(2,1)S(1)}, bf16[192,2048]{1,0:T(8,128)(2,1)}, u32[]{:S(2)}) %copy-start.1) | copy-done | bytes 786456
  1.3 0.7 copy-done.3
  2.0 0.3 prepare_integrals.1
  2.3 0.1 collective-permute-start
  2.4 1.7 %collective-permute-done = bf16[192,1024]{1,0:T(8,128)(2,1)S(1)} collective-permute-done((bf16[192,1024]{1,0:T(8,128)(2,1)S(1)}, bf16[192,1024]{1,0:T(8,128)(2,1)S(1)}, u32[]{:S(2)}, u32[]{:S(2)}) %collective-permute-start) | collective-permute-done | bytes 393248 | tf_op jit(solution)/shard_map/ppermute | solution.py:186
  4.3 1.6 %prepare_amplitudes.2 = bf16[512,1536]{1,0:T(8,128)(2,1)S(1)} custom-call(s32[4,24]{1,0:T(4,128)S(1)} %copy-done.4, bf16[512,3072]{1,0:T(8,128)(2,1)S(1)} %copy-done), custom_call_target="tpu_custom_call" | custom-call | bytes 4718592 | tf_op jit(solution)/shard_map/prepare_amplitudes/pallas_call | solution.py:104
  5.9 2.2 %collective-permute-start.1 = (bf16[512,1536]{1,0:T(8,128)(2,1)S(1)}, bf16[512,1536]{1,0:T(8,128)(2,1)S(1)}, u32[]{:S(2)}, u32[]{:S(2)}) collective-permute-start(bf16[512,1536]{1,0:T(8,128)(2,1)S(1)} %prepare_amplitudes.2), channel_id=1, source_target_pairs={{0,16},{8,24},{16,0},{24,8},{1,17},{9,25},{17,1},{25,9},{2,18},{10... | collective-permute-start | bytes 4718600 | tf_op jit(solution)/shard_map/ppermute | solution.py:190
  8.0 0.2 collective-permute-start.8
  8.2 3.9 %collective-permute-start.5 = (bf16[384,512]{1,0:T(8,128)(2,1)S(1)}, bf16[384,512]{1,0:T(8,128)(2,1)S(1)}, u32[]{:S(2)}, u32[]{:S(2)}) collective-permute-start(bf16[384,512]{1,0:T(8,128)(2,1)S(1)} %pad_maximum_fusion.1.refs_2_), channel_id=1, source_target_pairs={{0,224},{32,0},{64,32},{96,64},{128,96},{160,128},{192,160},{224,1... | collective-permute-start | bytes 1179656 | tf_op jit(solution)/shard_map/ppermute | solution.py:186
  12.1 2.0 %collective-permute-start.11 = (bf16[384,512]{1,0:T(8,128)(2,1)S(1)}, bf16[384,512]{1,0:T(8,128)(2,1)S(1)}, u32[]{:S(2)}, u32[]{:S(2)}) collective-permute-start(bf16[384,512]{1,0:T(8,128)(2,1)S(1)} %pad_maximum_fusion.2.refs_2_), channel_id=1, source_target_pairs={{0,224},{32,0},{64,32},{96,64},{128,96},{160,128},{192,160},{224,1... | collective-permute-start | bytes 1179656 | tf_op jit(solution)/shard_map/ppermute | solution.py:186
  14.2 0.0 collective-permute-start.2
  14.2 1.6 %prepare_amplitudes.3 = bf16[512,1536]{1,0:T(8,128)(2,1)S(1)} custom-call(s32[4,24]{1,0:T(4,128)S(1)} %copy-done.4, bf16[512,3072]{1,0:T(8,128)(2,1)S(1)} %copy-done), custom_call_target="tpu_custom_call" | custom-call | bytes 4718592 | tf_op jit(solution)/shard_map/prepare_amplitudes/pallas_call | solution.py:104
  15.7 6.3 %collective-permute-done.8.refs_3_ = bf16[384,512]{1,0:T(8,128)(2,1)S(1)} collective-permute-done((bf16[384,512]{1,0:T(8,128)(2,1)S(1)}, bf16[384,512]{1,0:T(8,128)(2,1)S(1)}, u32[]{:S(2)}, u32[]{:S(2)}) %collective-permute-start.8) | collective-permute-done | bytes 393248 | tf_op jit(solution)/shard_map/ppermute | solution.py:186
  22.1 0.0 collective-permute-start.9
  22.1 0.0 collective-permute-done.5.refs_4_
  22.1 3.3 %collective-permute-start.6 = (bf16[384,512]{1,0:T(8,128)(2,1)S(1)}, bf16[384,512]{1,0:T(8,128)(2,1)S(1)}, u32[]{:S(2)}, u32[]{:S(2)}) collective-permute-start(bf16[384,512]{1,0:T(8,128)(2,1)S(1)} %collective-permute-done.5.refs_4_), channel_id=1, source_target_pairs={{0,224},{32,0},{64,32},{96,64},{128,96},{160,128},{192,160},{224,1... | collective-permute-start | bytes 1179656 | tf_op jit(solution)/shard_map/ppermute | solution.py:186
  25.3 4.7 %collective-permute-done.11.refs_4_ = bf16[384,512]{1,0:T(8,128)(2,1)S(1)} collective-permute-done((bf16[384,512]{1,0:T(8,128)(2,1)S(1)}, bf16[384,512]{1,0:T(8,128)(2,1)S(1)}, u32[]{:S(2)}, u32[]{:S(2)}) %collective-permute-start.11) | collective-permute-done | bytes 393248 | tf_op jit(solution)/shard_map/ppermute | solution.py:186
  30.1 3.7 %collective-permute-start.12 = (bf16[384,512]{1,0:T(8,128)(2,1)S(1)}, bf16[384,512]{1,0:T(8,128)(2,1)S(1)}, u32[]{:S(2)}, u32[]{:S(2)}) collective-permute-start(bf16[384,512]{1,0:T(8,128)(2,1)S(1)} %collective-permute-done.11.refs_4_), channel_id=1, source_target_pairs={{0,224},{32,0},{64,32},{96,64},{128,96},{160,128},{192,160},{224,1... | collective-permute-start | bytes 1179656 | tf_op jit(solution)/shard_map/ppermute | solution.py:186
  33.8 0.0 collective-permute-done.2.refs_3_
  33.8 0.0 collective-permute-start.3
  33.8 5.2 %collective-permute-done.9.refs_5_ = bf16[384,512]{1,0:T(8,128)(2,1)S(1)} collective-permute-done((bf16[384,512]{1,0:T(8,128)(2,1)S(1)}, bf16[384,512]{1,0:T(8,128)(2,1)S(1)}, u32[]{:S(2)}, u32[]{:S(2)}) %collective-permute-start.9) | collective-permute-done | bytes 393248 | tf_op jit(solution)/shard_map/ppermute | solution.py:186
  38.9 0.0 collective-permute-start.10
  38.9 0.0 collective-permute-done.6.refs_6_
  38.9 3.3 %collective-permute-start.7 = (bf16[384,512]{1,0:T(8,128)(2,1)S(1)}, bf16[384,512]{1,0:T(8,128)(2,1)S(1)}, u32[]{:S(2)}, u32[]{:S(2)}) collective-permute-start(bf16[384,512]{1,0:T(8,128)(2,1)S(1)} %collective-permute-done.6.refs_6_), channel_id=1, source_target_pairs={{0,224},{32,0},{64,32},{96,64},{128,96},{160,128},{192,160},{224,1... | collective-permute-start | bytes 1179656 | tf_op jit(solution)/shard_map/ppermute | solution.py:186
  42.2 4.7 %collective-permute-done.12.refs_6_ = bf16[384,512]{1,0:T(8,128)(2,1)S(1)} collective-permute-done((bf16[384,512]{1,0:T(8,128)(2,1)S(1)}, bf16[384,512]{1,0:T(8,128)(2,1)S(1)}, u32[]{:S(2)}, u32[]{:S(2)}) %collective-permute-start.12) | collective-permute-done | bytes 393248 | tf_op jit(solution)/shard_map/ppermute | solution.py:186
  46.9 3.7 %collective-permute-start.13 = (bf16[384,512]{1,0:T(8,128)(2,1)S(1)}, bf16[384,512]{1,0:T(8,128)(2,1)S(1)}, u32[]{:S(2)}, u32[]{:S(2)}) collective-permute-start(bf16[384,512]{1,0:T(8,128)(2,1)S(1)} %collective-permute-done.12.refs_6_), channel_id=1, source_target_pairs={{0,224},{32,0},{64,32},{96,64},{128,96},{160,128},{192,160},{224,1... | collective-permute-start | bytes 1179656 | tf_op jit(solution)/shard_map/ppermute | solution.py:186
  50.6 0.0 collective-permute-done.1
  50.6 0.2 pad_maximum_fusion.refs_0_
  50.8 4.9 %collective-permute-done.10.refs_7_ = bf16[384,512]{1,0:T(8,128)(2,1)S(1)} collective-permute-done((bf16[384,512]{1,0:T(8,128)(2,1)S(1)}, bf16[384,512]{1,0:T(8,128)(2,1)S(1)}, u32[]{:S(2)}, u32[]{:S(2)}) %collective-permute-start.10) | collective-permute-done | bytes 393248 | tf_op jit(solution)/shard_map/ppermute | solution.py:186
  55.8 0.0 collective-permute-done.7.refs_8_
  55.8 7.0 %collective-permute-done.13.refs_8_ = bf16[384,512]{1,0:T(8,128)(2,1)S(1)} collective-permute-done((bf16[384,512]{1,0:T(8,128)(2,1)S(1)}, bf16[384,512]{1,0:T(8,128)(2,1)S(1)}, u32[]{:S(2)}, u32[]{:S(2)}) %collective-permute-start.13) | collective-permute-done | bytes 393248 | tf_op jit(solution)/shard_map/ppermute | solution.py:186
  62.8 0.7 collective-permute-done.4.refs_7_
  63.4 0.0 collective-permute-start.14
  63.4 3.0 %collective-permute-start.16 = (bf16[384,512]{1,0:T(8,128)(2,1)S(1)}, bf16[384,512]{1,0:T(8,128)(2,1)S(1)}, u32[]{:S(2)}, u32[]{:S(2)}) collective-permute-start(bf16[384,512]{1,0:T(8,128)(2,1)S(1)} %collective-permute-done.7.refs_8_), channel_id=1, source_target_pairs={{0,224},{32,0},{64,32},{96,64},{128,96},{160,128},{192,160},{224,1... | collective-permute-start | bytes 1179656 | tf_op jit(solution)/shard_map/ppermute | solution.py:186
  66.5 9.0 %collective-permute-done.16.refs_9_ = bf16[384,512]{1,0:T(8,128)(2,1)S(1)} collective-permute-done((bf16[384,512]{1,0:T(8,128)(2,1)S(1)}, bf16[384,512]{1,0:T(8,128)(2,1)S(1)}, u32[]{:S(2)}, u32[]{:S(2)}) %collective-permute-start.16) | collective-permute-done | bytes 393248 | tf_op jit(solution)/shard_map/ppermute | solution.py:186
  75.5 1.8 %product_c.1 = (f32[512,128]{1,0:T(8,128)S(1)}, f32[512,128]{1,0:T(8,128)S(1)}, f32[512,128]{1,0:T(8,128)S(1)}, f32[512,128]{1,0:T(8,128)S(1)}) custom-call(bf16[1024,1536]{1,0:T(8,128)(2,1)S(1)} %pad_maximum_fusion.refs_0_, bf16[1024,1536]{1,0:T(8,128)(2,1)S(1)} %collective-permute-done.14.refs_1_, bf16[384,512]{1,0:T(8,128)(2,1)S(1)} %pad_maximum_fusion.1.refs_2_, ...), custom_call_target="tpu_custom_call" | custom-call | flops 1610612736 | bytes 6291456 | tf_op jit(solution)/shard_map/product_c/pallas_call | solution.py:147
  77.3 1.6 %collective-permute-start.23 = (f32[512,128]{1,0:T(8,128)S(1)}, f32[512,128]{1,0:T(8,128)S(1)}, u32[]{:S(2)}, u32[]{:S(2)}) collective-permute-start(f32[512,128]{1,0:T(8,128)S(1)} %get-tuple-element.47), channel_id=1, source_target_pairs={{0,2},{2,4},{4,6},{6,0},{1,3},{3,5},{5,7},{7,1},{8,10},{10,12},{12... | collective-permute-start | bytes 786440 | tf_op jit(solution)/shard_map/ppermute | solution.py:186
  78.9 1.7 %collective-permute-start.24 = (f32[512,128]{1,0:T(8,128)S(1)}, f32[512,128]{1,0:T(8,128)S(1)}, u32[]{:S(2)}, u32[]{:S(2)}) collective-permute-start(f32[512,128]{1,0:T(8,128)S(1)} %get-tuple-element.48), channel_id=1, source_target_pairs={{0,6},{2,0},{4,2},{6,4},{1,7},{3,1},{5,3},{7,5},{8,14},{10,8},{12,... | collective-permute-start | bytes 786440 | tf_op jit(solution)/shard_map/ppermute | solution.py:186
  80.6 1.8 %product_b.1 = (f32[2,512,128]{2,1,0:T(8,128)S(1)}, f32[2,512,128]{2,1,0:T(8,128)S(1)}) custom-call(bf16[1024,1536]{1,0:T(8,128)(2,1)S(1)} %pad_maximum_fusion.refs_0_, bf16[1024,1536]{1,0:T(8,128)(2,1)S(1)} %collective-permute-done.14.refs_1_, bf16[384,512]{1,0:T(8,128)(2,1)S(1)} %pad_maximum_fusion.2.refs_2_, ...), custom_call_target="tpu_custom_call" | custom-call | flops 1610612736 | bytes 6291456 | tf_op jit(solution)/shard_map/product_b/pallas_call | solution.py:147
  82.4 0.4 collective-permute-start.26
  82.8 3.0 %collective-permute-start.27 = (f32[2,512,128]{2,1,0:T(8,128)S(1)}, f32[2,512,128]{2,1,0:T(8,128)S(1)}, u32[]{:S(2)}, u32[]{:S(2)}) collective-permute-start(f32[2,512,128]{2,1,0:T(8,128)S(1)} %get-tuple-element.51), channel_id=1, source_target_pairs={{0,6},{2,0},{4,2},{6,4},{1,7},{3,1},{5,3},{7,5},{8,14},{10,8},{12,... | collective-permute-start | bytes 1572872 | tf_op jit(solution)/shard_map/ppermute | solution.py:186
  85.7 1.8 %product_a.1 = (f32[512,128]{1,0:T(8,128)S(1)}, f32[512,128]{1,0:T(8,128)S(1)}, f32[512,128]{1,0:T(8,128)S(1)}, f32[512,128]{1,0:T(8,128)S(1)}) custom-call(bf16[1024,1536]{1,0:T(8,128)(2,1)S(1)} %pad_maximum_fusion.refs_0_, bf16[1024,1536]{1,0:T(8,128)(2,1)S(1)} %collective-permute-done.14.refs_1_, bf16[384,512]{1,0:T(8,128)(2,1)S(1)} %pad_maximum_fusion.1.refs_2_, ...), custom_call_target="tpu_custom_call" | custom-call | flops 1610612736 | bytes 6291456 | tf_op jit(solution)/shard_map/product_a/pallas_call | solution.py:147
  87.5 2.2 %collective-permute-start.17 = (f32[512,128]{1,0:T(8,128)S(1)}, f32[512,128]{1,0:T(8,128)S(1)}, u32[]{:S(2)}, u32[]{:S(2)}) collective-permute-start(f32[512,128]{1,0:T(8,128)S(1)} %get-tuple-element.41), channel_id=1, source_target_pairs={{0,8},{8,0},{16,24},{24,16},{1,9},{9,1},{17,25},{25,17},{2,10},{10... | collective-permute-start | bytes 786440 | tf_op jit(solution)/shard_map/ppermute | solution.py:190
  89.7 1.6 %collective-permute-start.18 = (f32[512,128]{1,0:T(8,128)S(1)}, f32[512,128]{1,0:T(8,128)S(1)}, u32[]{:S(2)}, u32[]{:S(2)}) collective-permute-start(f32[512,128]{1,0:T(8,128)S(1)} %get-tuple-element.42), channel_id=1, source_target_pairs={{0,24},{8,16},{16,8},{24,0},{1,25},{9,17},{17,9},{25,1},{2,26},{10... | collective-permute-start | bytes 786440 | tf_op jit(solution)/shard_map/ppermute | solution.py:190
  91.3 0.6 collective-permute-start.19
  91.9 1.8 %product_d.1 = (f32[512,128]{1,0:T(8,128)S(1)}, f32[512,128]{1,0:T(8,128)S(1)}, f32[512,128]{1,0:T(8,128)S(1)}, f32[512,128]{1,0:T(8,128)S(1)}) custom-call(bf16[1024,1536]{1,0:T(8,128)(2,1)S(1)} %pad_maximum_fusion.refs_0_, bf16[1024,1536]{1,0:T(8,128)(2,1)S(1)} %collective-permute-done.14.refs_1_, bf16[384,512]{1,0:T(8,128)(2,1)S(1)} %pad_maximum_fusion.2.refs_2_, ...), custom_call_target="tpu_custom_call" | custom-call | flops 1610612736 | bytes 6291456 | tf_op jit(solution)/shard_map/product_d/pallas_call | solution.py:147
  93.7 0.0 copy-start.2
  93.7 0.0 copy-start.5
  93.7 0.0 copy-start.6
  93.7 3.2 %collective-permute-done.17 = f32[512,128]{1,0:T(8,128)S(1)} collective-permute-done((f32[512,128]{1,0:T(8,128)S(1)}, f32[512,128]{1,0:T(8,128)S(1)}, u32[]{:S(2)}, u32[]{:S(2)}) %collective-permute-start.17) | collective-permute-done | bytes 262176 | tf_op jit(solution)/shard_map/ppermute | solution.py:190
  96.9 4.0 %collective-permute-done.18 = f32[512,128]{1,0:T(8,128)S(1)} collective-permute-done((f32[512,128]{1,0:T(8,128)S(1)}, f32[512,128]{1,0:T(8,128)S(1)}, u32[]{:S(2)}, u32[]{:S(2)}) %collective-permute-start.18) | collective-permute-done | bytes 262176 | tf_op jit(solution)/shard_map/ppermute | solution.py:190
  100.9 0.4 collective-permute-start.22
  101.3 0.6 collective-permute-done.19
  101.8 3.3 %collective-permute-start.25 = (f32[512,128]{1,0:T(8,128)S(1)}, f32[512,128]{1,0:T(8,128)S(1)}, u32[]{:S(2)}, u32[]{:S(2)}) collective-permute-start(f32[512,128]{1,0:T(8,128)S(1)} %add_add_fusion), channel_id=1, source_target_pairs={{0,16},{8,24},{16,0},{24,8},{1,17},{9,25},{17,1},{25,9},{2,18},{10... | collective-permute-start | bytes 786440 | tf_op jit(solution)/shard_map/ppermute | solution.py:190
  105.2 1.0 collective-permute-start.20
  106.1 0.1 fusion
  106.2 0.8 collective-permute-start.28
  107.0 0.3 collective-permute-start.29
  107.3 1.2 %collective-permute-done.22.refs_3_ = f32[512,128]{1,0:T(8,128)S(1)} collective-permute-done((f32[512,128]{1,0:T(8,128)S(1)}, f32[512,128]{1,0:T(8,128)S(1)}, u32[]{:S(2)}, u32[]{:S(2)}) %collective-permute-start.22) | collective-permute-done | bytes 262176 | tf_op jit(solution)/shard_map/ppermute | solution.py:186
  108.6 3.6 %collective-permute-done.25.refs_4_ = f32[512,128]{1,0:T(8,128)S(1)} collective-permute-done((f32[512,128]{1,0:T(8,128)S(1)}, f32[512,128]{1,0:T(8,128)S(1)}, u32[]{:S(2)}, u32[]{:S(2)}) %collective-permute-start.25) | collective-permute-done | bytes 262176 | tf_op jit(solution)/shard_map/ppermute | solution.py:190
  112.1 1.0 collective-permute-done.20.refs_1_
  113.1 0.6 collective-permute-done.28.refs_5_
  113.7 1.1 collective-permute-done.29.refs_6_
  114.8 0.9 finish.1
  (25 shorter events, 0.2 us)
Async XLA Ops:
  0.0 4.2 %copy-start = (bf16[512,3072]{1,0:T(8,128)(2,1)S(1)}, bf16[512,3072]{1,0:T(8,128)(2,1)}, u32[]{:S(2)}) copy-start(bf16[512,3072]{1,0:T(8,128)(2,1)} %in_ref.5) | copy-start | bytes 9437188
  0.0 1.3 %copy-start.1 = (bf16[192,2048]{1,0:T(8,128)(2,1)S(1)}, bf16[192,2048]{1,0:T(8,128)(2,1)}, u32[]{:S(2)}) copy-start(bf16[192,2048]{1,0:T(8,128)(2,1)} %in_ref.3) | copy-start | bytes 2359300
  1.3 0.7 copy-start.3
  2.0 2.2 %copy-start.4 = (s32[4,24]{1,0:T(4,128)S(1)}, s32[4,24]{1,0:T(4,128)}, u32[]{:S(2)}) copy-start(s32[4,24]{1,0:T(4,128)} %mask_ref.1) | copy-start | bytes 1156
  2.3 1.8 %collective-permute-start = (bf16[192,1024]{1,0:T(8,128)(2,1)S(1)}, bf16[192,1024]{1,0:T(8,128)(2,1)S(1)}, u32[]{:S(2)}, u32[]{:S(2)}) collective-permute-start(bf16[192,1024]{1,0:T(8,128)(2,1)S(1)} %get-tuple-element.30), channel_id=1, source_target_pairs={{0,1},{1,0},{2,3},{3,2},{4,5},{5,4},{6,7},{7,6},{8,9},{9,8},{10,11... | collective-permute-start | bytes 1179656 | tf_op jit(solution)/shard_map/ppermute | solution.py:186
  5.9 44.8 %collective-permute-start.1 = (bf16[512,1536]{1,0:T(8,128)(2,1)S(1)}, bf16[512,1536]{1,0:T(8,128)(2,1)S(1)}, u32[]{:S(2)}, u32[]{:S(2)}) collective-permute-start(bf16[512,1536]{1,0:T(8,128)(2,1)S(1)} %prepare_amplitudes.2), channel_id=1, source_target_pairs={{0,16},{8,24},{16,0},{24,8},{1,17},{9,25},{17,1},{25,9},{2,18},{10... | collective-permute-start | bytes 4718600 | tf_op jit(solution)/shard_map/ppermute | solution.py:190
  8.0 14.1 %collective-permute-start.8 = (bf16[384,512]{1,0:T(8,128)(2,1)S(1)}, bf16[384,512]{1,0:T(8,128)(2,1)S(1)}, u32[]{:S(2)}, u32[]{:S(2)}) collective-permute-start(bf16[384,512]{1,0:T(8,128)(2,1)S(1)} %pad_maximum_fusion.2.refs_2_), channel_id=1, source_target_pairs={{0,32},{32,64},{64,96},{96,128},{128,160},{160,192},{192,224},{224... | collective-permute-start | bytes 1179656 | tf_op jit(solution)/shard_map/ppermute | solution.py:186
  8.2 13.9 %collective-permute-start.5 = (bf16[384,512]{1,0:T(8,128)(2,1)S(1)}, bf16[384,512]{1,0:T(8,128)(2,1)S(1)}, u32[]{:S(2)}, u32[]{:S(2)}) collective-permute-start(bf16[384,512]{1,0:T(8,128)(2,1)S(1)} %pad_maximum_fusion.1.refs_2_), channel_id=1, source_target_pairs={{0,224},{32,0},{64,32},{96,64},{128,96},{160,128},{192,160},{224,1... | collective-permute-start | bytes 1179656 | tf_op jit(solution)/shard_map/ppermute | solution.py:186
  12.1 17.9 %collective-permute-start.11 = (bf16[384,512]{1,0:T(8,128)(2,1)S(1)}, bf16[384,512]{1,0:T(8,128)(2,1)S(1)}, u32[]{:S(2)}, u32[]{:S(2)}) collective-permute-start(bf16[384,512]{1,0:T(8,128)(2,1)S(1)} %pad_maximum_fusion.2.refs_2_), channel_id=1, source_target_pairs={{0,224},{32,0},{64,32},{96,64},{128,96},{160,128},{192,160},{224,1... | collective-permute-start | bytes 1179656 | tf_op jit(solution)/shard_map/ppermute | solution.py:186
  14.2 19.6 %collective-permute-start.2 = (bf16[384,512]{1,0:T(8,128)(2,1)S(1)}, bf16[384,512]{1,0:T(8,128)(2,1)S(1)}, u32[]{:S(2)}, u32[]{:S(2)}) collective-permute-start(bf16[384,512]{1,0:T(8,128)(2,1)S(1)} %pad_maximum_fusion.1.refs_2_), channel_id=1, source_target_pairs={{0,32},{32,64},{64,96},{96,128},{128,160},{160,192},{192,224},{224... | collective-permute-start | bytes 1179656 | tf_op jit(solution)/shard_map/ppermute | solution.py:186
  22.1 16.9 %collective-permute-start.9 = (bf16[384,512]{1,0:T(8,128)(2,1)S(1)}, bf16[384,512]{1,0:T(8,128)(2,1)S(1)}, u32[]{:S(2)}, u32[]{:S(2)}) collective-permute-start(bf16[384,512]{1,0:T(8,128)(2,1)S(1)} %collective-permute-done.8.refs_3_), channel_id=1, source_target_pairs={{0,32},{32,64},{64,96},{96,128},{128,160},{160,192},{192,224},{224... | collective-permute-start | bytes 1179656 | tf_op jit(solution)/shard_map/ppermute | solution.py:186
  22.1 16.9 %collective-permute-start.6 = (bf16[384,512]{1,0:T(8,128)(2,1)S(1)}, bf16[384,512]{1,0:T(8,128)(2,1)S(1)}, u32[]{:S(2)}, u32[]{:S(2)}) collective-permute-start(bf16[384,512]{1,0:T(8,128)(2,1)S(1)} %collective-permute-done.5.refs_4_), channel_id=1, source_target_pairs={{0,224},{32,0},{64,32},{96,64},{128,96},{160,128},{192,160},{224,1... | collective-permute-start | bytes 1179656 | tf_op jit(solution)/shard_map/ppermute | solution.py:186
  30.1 16.9 %collective-permute-start.12 = (bf16[384,512]{1,0:T(8,128)(2,1)S(1)}, bf16[384,512]{1,0:T(8,128)(2,1)S(1)}, u32[]{:S(2)}, u32[]{:S(2)}) collective-permute-start(bf16[384,512]{1,0:T(8,128)(2,1)S(1)} %collective-permute-done.11.refs_4_), channel_id=1, source_target_pairs={{0,224},{32,0},{64,32},{96,64},{128,96},{160,128},{192,160},{224,1... | collective-permute-start | bytes 1179656 | tf_op jit(solution)/shard_map/ppermute | solution.py:186
  33.8 16.9 %collective-permute-start.3 = (bf16[384,512]{1,0:T(8,128)(2,1)S(1)}, bf16[384,512]{1,0:T(8,128)(2,1)S(1)}, u32[]{:S(2)}, u32[]{:S(2)}) collective-permute-start(bf16[384,512]{1,0:T(8,128)(2,1)S(1)} %collective-permute-done.2.refs_3_), channel_id=1, source_target_pairs={{0,32},{32,64},{64,96},{96,128},{128,160},{160,192},{192,224},{224... | collective-permute-start | bytes 1179656 | tf_op jit(solution)/shard_map/ppermute | solution.py:186
  38.9 16.9 %collective-permute-start.10 = (bf16[384,512]{1,0:T(8,128)(2,1)S(1)}, bf16[384,512]{1,0:T(8,128)(2,1)S(1)}, u32[]{:S(2)}, u32[]{:S(2)}) collective-permute-start(bf16[384,512]{1,0:T(8,128)(2,1)S(1)} %collective-permute-done.9.refs_5_), channel_id=1, source_target_pairs={{0,32},{32,64},{64,96},{96,128},{128,160},{160,192},{192,224},{224... | collective-permute-start | bytes 1179656 | tf_op jit(solution)/shard_map/ppermute | solution.py:186
  38.9 16.8 %collective-permute-start.7 = (bf16[384,512]{1,0:T(8,128)(2,1)S(1)}, bf16[384,512]{1,0:T(8,128)(2,1)S(1)}, u32[]{:S(2)}, u32[]{:S(2)}) collective-permute-start(bf16[384,512]{1,0:T(8,128)(2,1)S(1)} %collective-permute-done.6.refs_6_), channel_id=1, source_target_pairs={{0,224},{32,0},{64,32},{96,64},{128,96},{160,128},{192,160},{224,1... | collective-permute-start | bytes 1179656 | tf_op jit(solution)/shard_map/ppermute | solution.py:186
  46.9 15.9 %collective-permute-start.13 = (bf16[384,512]{1,0:T(8,128)(2,1)S(1)}, bf16[384,512]{1,0:T(8,128)(2,1)S(1)}, u32[]{:S(2)}, u32[]{:S(2)}) collective-permute-start(bf16[384,512]{1,0:T(8,128)(2,1)S(1)} %collective-permute-done.12.refs_6_), channel_id=1, source_target_pairs={{0,224},{32,0},{64,32},{96,64},{128,96},{160,128},{192,160},{224,1... | collective-permute-start | bytes 1179656 | tf_op jit(solution)/shard_map/ppermute | solution.py:186
  50.6 12.8 %collective-permute-start.4 = (bf16[384,512]{1,0:T(8,128)(2,1)S(1)}, bf16[384,512]{1,0:T(8,128)(2,1)S(1)}, u32[]{:S(2)}, u32[]{:S(2)}) collective-permute-start(bf16[384,512]{1,0:T(8,128)(2,1)S(1)} %collective-permute-done.3.refs_5_), channel_id=1, source_target_pairs={{0,32},{32,64},{64,96},{96,128},{128,160},{160,192},{192,224},{224... | collective-permute-start | bytes 1179656 | tf_op jit(solution)/shard_map/ppermute | solution.py:186
  63.4 12.1 %collective-permute-start.14 = (bf16[1024,1536]{1,0:T(8,128)(2,1)S(1)}, bf16[1024,1536]{1,0:T(8,128)(2,1)S(1)}, u32[]{:S(2)}, u32[]{:S(2)}) collective-permute-start(bf16[1024,1536]{1,0:T(8,128)(2,1)S(1)} %pad_maximum_fusion.refs_0_), channel_id=1, source_target_pairs={{0,1},{1,0},{2,3},{3,2},{4,5},{5,4},{6,7},{7,6},{8,9},{9,8},{10,11... | collective-permute-start | bytes 9437192 | tf_op jit(solution)/shard_map/ppermute | solution.py:186
  63.4 12.1 %collective-permute-start.16 = (bf16[384,512]{1,0:T(8,128)(2,1)S(1)}, bf16[384,512]{1,0:T(8,128)(2,1)S(1)}, u32[]{:S(2)}, u32[]{:S(2)}) collective-permute-start(bf16[384,512]{1,0:T(8,128)(2,1)S(1)} %collective-permute-done.7.refs_8_), channel_id=1, source_target_pairs={{0,224},{32,0},{64,32},{96,64},{128,96},{160,128},{192,160},{224,1... | collective-permute-start | bytes 1179656 | tf_op jit(solution)/shard_map/ppermute | solution.py:186
  66.5 14.2 %collective-permute-start.15 = (bf16[384,512]{1,0:T(8,128)(2,1)S(1)}, bf16[384,512]{1,0:T(8,128)(2,1)S(1)}, u32[]{:S(2)}, u32[]{:S(2)}) collective-permute-start(bf16[384,512]{1,0:T(8,128)(2,1)S(1)} %collective-permute-done.10.refs_7_), channel_id=1, source_target_pairs={{0,32},{32,64},{64,96},{96,128},{128,160},{160,192},{192,224},{224... | collective-permute-start | bytes 1179656 | tf_op jit(solution)/shard_map/ppermute | solution.py:186
  77.3 12.4 %collective-permute-start.23 = (f32[512,128]{1,0:T(8,128)S(1)}, f32[512,128]{1,0:T(8,128)S(1)}, u32[]{:S(2)}, u32[]{:S(2)}) collective-permute-start(f32[512,128]{1,0:T(8,128)S(1)} %get-tuple-element.47), channel_id=1, source_target_pairs={{0,2},{2,4},{4,6},{6,0},{1,3},{3,5},{5,7},{7,1},{8,10},{10,12},{12... | collective-permute-start | bytes 786440 | tf_op jit(solution)/shard_map/ppermute | solution.py:186
  78.9 12.4 %collective-permute-start.24 = (f32[512,128]{1,0:T(8,128)S(1)}, f32[512,128]{1,0:T(8,128)S(1)}, u32[]{:S(2)}, u32[]{:S(2)}) collective-permute-start(f32[512,128]{1,0:T(8,128)S(1)} %get-tuple-element.48), channel_id=1, source_target_pairs={{0,6},{2,0},{4,2},{6,4},{1,7},{3,1},{5,3},{7,5},{8,14},{10,8},{12,... | collective-permute-start | bytes 786440 | tf_op jit(solution)/shard_map/ppermute | solution.py:186
  82.4 22.7 %collective-permute-start.26 = (f32[2,512,128]{2,1,0:T(8,128)S(1)}, f32[2,512,128]{2,1,0:T(8,128)S(1)}, u32[]{:S(2)}, u32[]{:S(2)}) collective-permute-start(f32[2,512,128]{2,1,0:T(8,128)S(1)} %get-tuple-element.50), channel_id=1, source_target_pairs={{0,2},{2,4},{4,6},{6,0},{1,3},{3,5},{5,7},{7,1},{8,10},{10,12},{12... | collective-permute-start | bytes 1572872 | tf_op jit(solution)/shard_map/ppermute | solution.py:186
  82.8 23.3 %collective-permute-start.27 = (f32[2,512,128]{2,1,0:T(8,128)S(1)}, f32[2,512,128]{2,1,0:T(8,128)S(1)}, u32[]{:S(2)}, u32[]{:S(2)}) collective-permute-start(f32[2,512,128]{2,1,0:T(8,128)S(1)} %get-tuple-element.51), channel_id=1, source_target_pairs={{0,6},{2,0},{4,2},{6,4},{1,7},{3,1},{5,3},{7,5},{8,14},{10,8},{12,... | collective-permute-start | bytes 1572872 | tf_op jit(solution)/shard_map/ppermute | solution.py:186
  87.5 9.4 %collective-permute-start.17 = (f32[512,128]{1,0:T(8,128)S(1)}, f32[512,128]{1,0:T(8,128)S(1)}, u32[]{:S(2)}, u32[]{:S(2)}) collective-permute-start(f32[512,128]{1,0:T(8,128)S(1)} %get-tuple-element.41), channel_id=1, source_target_pairs={{0,8},{8,0},{16,24},{24,16},{1,9},{9,1},{17,25},{25,17},{2,10},{10... | collective-permute-start | bytes 786440 | tf_op jit(solution)/shard_map/ppermute | solution.py:190
  89.7 11.3 %collective-permute-start.18 = (f32[512,128]{1,0:T(8,128)S(1)}, f32[512,128]{1,0:T(8,128)S(1)}, u32[]{:S(2)}, u32[]{:S(2)}) collective-permute-start(f32[512,128]{1,0:T(8,128)S(1)} %get-tuple-element.42), channel_id=1, source_target_pairs={{0,24},{8,16},{16,8},{24,0},{1,25},{9,17},{17,9},{25,1},{2,26},{10... | collective-permute-start | bytes 786440 | tf_op jit(solution)/shard_map/ppermute | solution.py:190
  91.3 10.6 %collective-permute-start.19 = (f32[512,128]{1,0:T(8,128)S(1)}, f32[512,128]{1,0:T(8,128)S(1)}, u32[]{:S(2)}, u32[]{:S(2)}) collective-permute-start(f32[512,128]{1,0:T(8,128)S(1)} %get-tuple-element.43), channel_id=1, source_target_pairs={{0,16},{8,24},{16,0},{24,8},{1,17},{9,25},{17,1},{25,9},{2,18},{10... | collective-permute-start | bytes 786440 | tf_op jit(solution)/shard_map/ppermute | solution.py:190
  93.7 21.1 %copy-start.2 = (f32[128,512]{1,0:T(8,128)S(1)}, f32[128,512]{1,0:T(8,128)}, u32[]{:S(2)}) copy-start(f32[128,512]{1,0:T(8,128)} %refs_7_.1) | copy-start | bytes 786436
  93.7 21.1 %copy-start.5 = (f32[512]{0:T(512)S(1)}, f32[512]{0:T(512)}, u32[]{:S(2)}) copy-start(f32[512]{0:T(512)} %param.12) | copy-start | bytes 6148
  93.7 21.1 %copy-start.6 = (f32[128]{0:T(128)S(1)}, f32[128]{0:T(128)}, u32[]{:S(2)}) copy-start(f32[128]{0:T(128)} %param.13) | copy-start | bytes 1540
  96.9 10.1 %collective-permute-start.21 = (f32[512,128]{1,0:T(8,128)S(1)}, f32[512,128]{1,0:T(8,128)S(1)}, u32[]{:S(2)}, u32[]{:S(2)}) collective-permute-start(f32[512,128]{1,0:T(8,128)S(1)} %get-tuple-element.44), channel_id=1, source_target_pairs={{0,2},{2,4},{4,6},{6,0},{1,3},{3,5},{5,7},{7,1},{8,10},{10,12},{12... | collective-permute-start | bytes 786440 | tf_op jit(solution)/shard_map/ppermute | solution.py:186
  100.9 7.6 %collective-permute-start.22 = (f32[512,128]{1,0:T(8,128)S(1)}, f32[512,128]{1,0:T(8,128)S(1)}, u32[]{:S(2)}, u32[]{:S(2)}) collective-permute-start(f32[512,128]{1,0:T(8,128)S(1)} %get-tuple-element.45), channel_id=1, source_target_pairs={{0,6},{2,0},{4,2},{6,4},{1,7},{3,1},{5,3},{7,5},{8,14},{10,8},{12,... | collective-permute-start | bytes 786440 | tf_op jit(solution)/shard_map/ppermute | solution.py:186
  101.8 10.3 %collective-permute-start.25 = (f32[512,128]{1,0:T(8,128)S(1)}, f32[512,128]{1,0:T(8,128)S(1)}, u32[]{:S(2)}, u32[]{:S(2)}) collective-permute-start(f32[512,128]{1,0:T(8,128)S(1)} %add_add_fusion), channel_id=1, source_target_pairs={{0,16},{8,24},{16,0},{24,8},{1,17},{9,25},{17,1},{25,9},{2,18},{10... | collective-permute-start | bytes 786440 | tf_op jit(solution)/shard_map/ppermute | solution.py:190
  105.2 8.0 %collective-permute-start.20 = (f32[512,128]{1,0:T(8,128)S(1)}, f32[512,128]{1,0:T(8,128)S(1)}, u32[]{:S(2)}, u32[]{:S(2)}) collective-permute-start(f32[512,128]{1,0:T(8,128)S(1)} %add_add_fusion.1), channel_id=1, source_target_pairs={{0,4},{2,6},{4,0},{6,2},{1,5},{3,7},{5,1},{7,3},{8,12},{10,14},{12... | collective-permute-start | bytes 786440 | tf_op jit(solution)/shard_map/ppermute | solution.py:186
  106.2 7.5 %collective-permute-start.28 = (f32[512,128]{1,0:T(8,128)S(1)}, f32[512,128]{1,0:T(8,128)S(1)}, u32[]{:S(2)}, u32[]{:S(2)}) collective-permute-start(f32[512,128]{1,0:T(8,128)S(1)} %get-tuple-element.54), channel_id=1, source_target_pairs={{0,8},{8,0},{16,24},{24,16},{1,9},{9,1},{17,25},{25,17},{2,10},{10... | collective-permute-start | bytes 786440 | tf_op jit(solution)/shard_map/ppermute | solution.py:190
  107.0 7.8 %collective-permute-start.29 = (f32[512,128]{1,0:T(8,128)S(1)}, f32[512,128]{1,0:T(8,128)S(1)}, u32[]{:S(2)}, u32[]{:S(2)}) collective-permute-start(f32[512,128]{1,0:T(8,128)S(1)} %get-tuple-element.53), channel_id=1, source_target_pairs={{0,24},{8,16},{16,8},{24,0},{1,25},{9,17},{17,9},{25,1},{2,26},{10... | collective-permute-start | bytes 786440 | tf_op jit(solution)/shard_map/ppermute | solution.py:190
